TPU v7x, 32 devices: a whole 2x2x4 slice. The times are simulated.
32 devices in a mesh: groups: 2 (over x), ctx: 8 (over z, y), tp: 2 (over core).
Axes of the slice: x: 2, y: 2, z: 4, core: 2. Of those that a mesh axis runs over, the one named last changes fastest.
Arguments:
- queries: bfloat16 [3072, 4096], P(('groups', 'ctx'), 'tp'), parts along dimension 0, may hold values from -8 to 8
- keys: bfloat16 [3072, 512], P(('groups', 'ctx'), 'tp'), parts along dimension 0, may hold values from -8 to 8
- values: bfloat16 [3072, 512], P(('groups', 'ctx'), 'tp'), parts along dimension 0, may hold values from -6 to 6
- segments: int32 [3072], P(('groups', 'ctx')), parts along dimension 0, may hold values from 0 to 7, never falling along the last dimension, each value on 1 to 768 neighbouring positions
- valid_length: int32 [2], P('groups'), parts along dimension 0, may hold values from 768 to 1536
- reward_weight: float32 [4096], P('tp'), may hold values from -0.09375 to 0.09375
Outputs:
- attention: bfloat16 [3072, 4096], P(('groups', 'ctx'), 'tp'), parts along dimension 0
- reward: float32 [3072], P(('groups', 'ctx')), parts along dimension 0
There are 2 independent parts, one for each index of `groups`. A program takes and returns all parts, laid end to end along the dimension named above; an argument that names none is the same for every part. Nothing has to cross between parts.
Inputs may be any that keep to these rules, and one draw needn't show every extreme that they name: `segments`: ids never fall along positions; each document spans at most 768 positions.
All inputs are finite; a program needn't handle non-finite values.
Results may differ from a plain program's by a relative error of at most 0.0061.
Values may be sent and summed in bfloat16 or wider, within the bound.
A program may use at most 128 MiB of HBM per device.

v0:
```python
import math

import jax
import jax.numpy as jnp
from jax import lax
from jax.sharding import PartitionSpec as P

HEAD = 128


def rotate(matrix, positions, heads):
    row_count = matrix.shape[0]
    half_dim = HEAD // 2
    entries = matrix.astype(jnp.float32).reshape(row_count, heads, HEAD)
    steps_index = jnp.arange(half_dim).astype(jnp.float32)
    frequency = jnp.exp(steps_index * (-2.0 * math.log(1000000.0) / HEAD))
    angles = positions.astype(jnp.float32)[:, None] * frequency[None, :]
    cosine = jnp.cos(angles)[:, None, :]
    sine = jnp.sin(angles)[:, None, :]
    lower = entries[..., :half_dim]
    upper = entries[..., half_dim:]
    turned = jnp.concatenate(
        [lower * cosine - upper * sine, upper * cosine + lower * sine], axis=-1
    )
    return turned.reshape(row_count, heads * HEAD).astype(jnp.bfloat16)


def attend(
    carry_state,
    query_rows,
    query_pos,
    query_doc,
    key_rows,
    value_rows,
    key_pos,
    key_doc,
    valid_rows,
):
    running_max, running_sum, running_out = carry_state
    kv_heads = key_rows.shape[1] // HEAD
    row_count = query_rows.shape[0]
    group_size = query_rows.shape[1] // HEAD // kv_heads
    piece_rows = key_rows.shape[0]
    query_four = query_rows.reshape(row_count, kv_heads, group_size, HEAD)
    key_three = key_rows.reshape(piece_rows, kv_heads, HEAD)
    value_three = value_rows.reshape(piece_rows, kv_heads, HEAD)
    scores = jnp.einsum(
        "rkgd,skd->kgrs", query_four, key_three, preferred_element_type=jnp.float32
    ) * HEAD ** (-0.5)
    allowed = (key_doc[None, :] == query_doc[:, None]) & (key_pos[None, :] <= query_pos[:, None])
    allowed = allowed & ((key_pos[None, :] < valid_rows) | (key_pos[None, :] == query_pos[:, None]))
    masked = jnp.where(allowed, scores, -jnp.inf)
    new_max = jnp.maximum(running_max, jnp.max(masked, axis=-1))
    weights = jnp.where(allowed, jnp.exp(scores - new_max[..., None]), 0.0)
    new_sum = jnp.sum(weights, axis=-1)
    mixed = jnp.einsum(
        "kgrs,skd->kgrd",
        weights.astype(jnp.bfloat16),
        value_three,
        preferred_element_type=jnp.float32,
    )
    return (new_max, new_sum, mixed)


def finish(carry_state, query_pos, valid_rows):
    running_max, running_sum, running_out = carry_state
    normed = running_out / running_sum[..., None]
    row_count = normed.shape[2]
    flat = jnp.transpose(normed, (2, 0, 1, 3)).reshape(row_count, -1)
    return flat * (query_pos < valid_rows).astype(jnp.float32)[:, None]


def per_device(queries, keys, values, segments, valid_length, reward_weight):
    row_count = queries.shape[0]
    half_rows = row_count // 2
    my_index = lax.axis_index("ctx")
    positions = my_index * row_count + jnp.arange(row_count, dtype=jnp.int32)
    q_heads = queries.shape[1] // HEAD
    kv_heads = keys.shape[1] // HEAD
    group_size = q_heads // kv_heads
    q_rot = rotate(queries, positions, q_heads)
    k_rot = rotate(keys, positions, kv_heads)
    doc_all = lax.all_gather(segments, "ctx", axis=0, tiled=True)
    valid_rows = valid_length[0]
    first_rows = q_rot[:half_rows]
    first_pos = positions[:half_rows]
    second_rows = q_rot[half_rows:]
    second_pos = positions[half_rows:]
    first_doc = lax.dynamic_slice_in_dim(doc_all, first_pos[0], half_rows)
    second_doc = lax.dynamic_slice_in_dim(doc_all, second_pos[0], half_rows)

    def empty_state():
        return (
            jnp.full((kv_heads, group_size, half_rows), -1e30, jnp.float32),
            jnp.zeros((kv_heads, group_size, half_rows), jnp.float32),
            jnp.zeros((kv_heads, group_size, half_rows, HEAD), jnp.float32),
        )

    begin_row = jnp.int32(0)
    key_rows = lax.all_gather(k_rot, "ctx", axis=0, tiled=True)
    value_rows = lax.all_gather(values, "ctx", axis=0, tiled=True)
    piece_rows = key_rows.shape[0]
    key_pos = jnp.arange(piece_rows, dtype=jnp.int32)

    def first_step(carry_state):
        return attend(
            carry_state,
            first_rows,
            first_pos,
            first_doc,
            key_rows,
            value_rows,
            key_pos,
            doc_all,
            valid_rows,
        )

    def second_step(carry_state):
        return attend(
            carry_state,
            second_rows,
            second_pos,
            second_doc,
            key_rows,
            value_rows,
            key_pos,
            doc_all,
            valid_rows,
        )

    def keep_state(carry_state):
        return carry_state

    first_needed = (begin_row <= first_pos[-1]) & (doc_all[-1] >= first_doc[0])
    second_needed = (begin_row <= second_pos[-1]) & (doc_all[-1] >= second_doc[0])
    new_first = lax.cond(first_needed, first_step, keep_state, empty_state())
    new_second = lax.cond(second_needed, second_step, keep_state, empty_state())
    outputs = jnp.concatenate(
        [finish(new_first, first_pos, valid_rows), finish(new_second, second_pos, valid_rows)],
        axis=0,
    )
    partial_reward = jnp.dot(outputs, reward_weight, precision=lax.Precision.HIGHEST)
    reward = lax.psum(partial_reward, "tp")
    attention = outputs.astype(jnp.bfloat16)
    return (attention, reward)


def solution(mesh):
    return jax.shard_map(
        per_device,
        mesh=mesh,
        in_specs=(
            P(("groups", "ctx"), "tp"),
            P(("groups", "ctx"), "tp"),
            P(("groups", "ctx"), "tp"),
            P(("groups", "ctx")),
            P("groups"),
            P("tp"),
        ),
        out_specs=(P(("groups", "ctx"), "tp"), P(("groups", "ctx"))),
        check_vma=False,
    )
```

profile of v0, /device:TPU:0, one launch (start us, length us, event | category | flops | bytes accessed | tf_op | source)
XLA Modules:
  0.0 141.6 jit_solution(14540691396740771923)
XLA Ops:
  0.6 0.0 copy-start
  0.6 0.0 copy-start.4
  0.7 0.0 copy-start.3
  0.7 0.6 fusion.34
  5.2 1.2 dynamic-slice
  7.1 0.9 dynamic-update-slice
  8.0 13.2 %all-reduce = s32[1536]{0:T(1024)S(1)} all-reduce(s32[1536]{0:T(1024)S(1)} %dynamic-update-slice), channel_id=1, replica_groups=mesh['groups'=2,'ctx'=8,'tp'=2] {'ctx'}, use_global_device_ids=true, to_apply=%add | all-reduce | flops 1536 | bytes 12288
  21.2 0.1 fusion.32
  21.3 0.4 multiply_cosine_fusion
  21.7 1.3 convert_bitcast_fusion
  23.0 0.3 copy.37
  23.3 0.7 subtract_convert_fusion
  24.1 0.4 pad_maximum_fusion.2
  24.5 1.1 copy.65
  25.6 0.0 copy-done.4
  25.6 0.1 reshape.144
  25.7 0.5 subtract_convert_fusion.1
  26.2 0.3 pad_maximum_fusion.3
  26.5 32.5 %all_gather.10 = bf16[1536,256]{1,0:T(8,128)(2,1)S(1)} all-gather(bf16[192,256]{1,0:T(8,128)(2,1)S(1)} %bitcast.92), channel_id=1, replica_groups=mesh['groups'=2,'ctx'=8,'tp'=2] {'ctx'}, dimensions={0}, use_global_device_ids=true | all-gather | bytes 884736 | tf_op jit(solution)/shard_map/all_gather | solution.py:100
  59.0 0.1 fusion.33
  59.1 0.0 copy-done.3
  59.1 31.7 %all_gather.11 = bf16[1536,256]{1,0:T(8,128)(2,1)S(1)} all-gather(bf16[192,256]{1,0:T(8,128)(2,1)S(1)} %copy-done.3), channel_id=1, replica_groups=mesh['groups'=2,'ctx'=8,'tp'=2] {'ctx'}, dimensions={0}, use_global_device_ids=true | all-gather | bytes 884736 | tf_op jit(solution)/shard_map/all_gather | solution.py:101
  90.7 0.6 slice.65
  92.5 17.7 %conditional.2 = (f32[2,8,96]{2,1,0:T(8,128)S(1)}, f32[2,8,96,128]{3,2,1,0:T(8,128)}) conditional(s32[]{:T(128)} %bitcast.8, () %tuple.24, (s32[1536]{0:T(1024)S(1)}, s32[96]{0:T(128)S(1)}, s32[1536]{0:T(1024)S(1)}, s32[1536]{0:T(1024)S(1)}, s32[96]{0:T(128)S(1)}, /*index=5*/s32[]{:T(128)}, s32[1536]{0:T(1024)S(1)}, bf16[1536,256]{1,0:T(8,128)(2,1)S(1)}, ...), branch_computations={%region_0.0_spmd, %region_1.4_spmd} | conditional | flops 1234796544 | bytes 64749404 | solution.py:136
  92.5 0.7 broadcast_compare_fusion
  93.2 0.3 or_and_fusion
  93.5 0.2 reshape.124
  93.7 1.0 slice_bitcast_fusion
  94.7 0.1 copy.34
  94.8 5.3 %fusion = (f32[2,8,96]{2,1,0:T(8,128)S(1)}, f32[2,1536,96,8]{1,2,3,0:T(8,128)}) fusion(pred[96,1536]{1,0:T(8,128)(4,1)S(1)} %or_and_fusion, bf16[96,2,8,128]{3,2,1,0:T(8,128)(2,1)S(1)} %bitcast.88, bf16[1536,2,128,1]{2,1,0,3:T(2,128)(2,1)S(1)} %bitcast.81), kind=kOutput, calls=%fused_computation.2 | convolution fusion | flops 611056128 | bytes 10770432 | tf_op jit(solution)/shard_map/cond/branch_1_fun/rkgd,skd->kgrs/dot_general | solution.py:47
  100.0 0.0 slice-start
  100.1 1.1 reshape.126
  101.1 6.6 %fusion.5 = f32[2,8,96,128]{3,2,1,0:T(8,128)} fusion(f32[2,1536,96,8]{1,2,3,0:T(8,128)} %get-tuple-element.69, f32[2,8,96]{2,1,0:T(8,128)S(1)} %broadcast_maximum_fusion, pred[96,1536]{1,0:T(8,128)(4,1)S(1)} %or_and_fusion, bf16[1536,2,128,1]{2,1,0,3:T(2,128)(2,1)} %bitcast.90), kind=kOutput, calls=%fused_computation.7 | convolution fusion | flops 613416960 | bytes 11163648 | tf_op jit(solution)/shard_map/cond/branch_1_fun/kgrs,skd->kgrd/dot_general | solution.py:56
  107.7 0.0 slice-done
  107.7 0.0 slice-done.1
  107.7 0.0 slice-done.2
  107.7 2.5 %fusion.4 = f32[2,8,96]{2,1,0:T(8,128)S(1)} fusion(f32[2,1536,96,8]{1,2,3,0:T(8,128)S(1)} %bitcast.77, f32[2,8,96]{2,1,0:T(8,128)S(1)} %broadcast_maximum_fusion, pred[96,1536]{1,0:T(8,128)(4,1)S(1)} %or_and_fusion), kind=kLoop, calls=%fused_computation.6 | loop fusion | flops 9435648 | bytes 9596928 | tf_op jit(solution)/shard_map/cond/branch_1_fun/reduce_sum | solution.py:55
  110.2 1.4 divide_bitcast_fusion.1
  111.6 0.5 copy.20
  112.7 0.1 compare_convert_fusion.1
  112.8 0.3 bitcast_multiply_fusion.1
  114.3 19.7 %conditional.3 = (f32[2,8,96]{2,1,0:T(8,128)S(1)}, f32[2,8,96,128]{3,2,1,0:T(8,128)}) conditional(s32[]{:T(128)} %bitcast.12, () %tuple.26, (s32[1536]{0:T(1024)S(1)}, s32[96]{0:T(128)S(1)}, s32[1536]{0:T(1024)S(1)}, s32[1536]{0:T(1024)S(1)}, s32[96]{0:T(128)S(1)}, /*index=5*/s32[]{:T(128)}, s32[1536]{0:T(1024)S(1)}, bf16[1536,256]{1,0:T(8,128)(2,1)S(1)}, ...), branch_computations={%region_4.5_spmd, %region_5.8_spmd} | conditional | flops 1234796544 | bytes 65929108 | solution.py:137
  114.5 0.7 broadcast_compare_fusion.1
  115.2 0.3 or_and_fusion.1
  115.5 0.0 copy-start.1
  115.5 1.1 slice_bitcast_fusion.1
  116.6 0.8 copy.35
  117.4 0.2 reshape.127
  117.6 0.0 copy-done.1
  117.6 6.3 %fusion.14 = (f32[2,8,96]{2,1,0:T(8,128)S(1)}, f32[2,1536,96,8]{1,2,3,0:T(8,128)}) fusion(pred[96,1536]{1,0:T(8,128)(4,1)S(1)} %or_and_fusion.1, bf16[96,2,8,128]{3,2,1,0:T(8,128)(2,1)} %bitcast.89, bf16[1536,2,128,1]{2,1,0,3:T(2,128)(2,1)S(1)} %bitcast.82), kind=kOutput, calls=%fused_computation.21 | convolution fusion | flops 611056128 | bytes 10770432 | tf_op jit(solution)/shard_map/cond/branch_1_fun/rkgd,skd->kgrs/dot_general | solution.py:47
  123.9 1.1 reshape.129
  124.9 6.6 %fusion.19 = f32[2,8,96,128]{3,2,1,0:T(8,128)} fusion(f32[2,1536,96,8]{1,2,3,0:T(8,128)} %get-tuple-element.71, f32[2,8,96]{2,1,0:T(8,128)S(1)} %broadcast_maximum_fusion.1, pred[96,1536]{1,0:T(8,128)(4,1)} %copy-done.1, bf16[1536,2,128,1]{2,1,0,3:T(2,128)(2,1)} %bitcast.91), kind=kOutput, calls=%fused_computation.26 | convolution fusion | flops 613416960 | bytes 11163648 | tf_op jit(solution)/shard_map/cond/branch_1_fun/kgrs,skd->kgrd/dot_general | solution.py:56
  131.6 0.0 slice-done.3
  131.6 0.0 copy-done.2
  131.6 0.0 slice-done.4
  131.6 0.0 slice-done.5
  131.6 2.5 %fusion.18 = f32[2,8,96]{2,1,0:T(8,128)S(1)} fusion(f32[2,1536,96,8]{1,2,3,0:T(8,128)S(1)} %bitcast.79, f32[2,8,96]{2,1,0:T(8,128)S(1)} %broadcast_maximum_fusion.1, pred[96,1536]{1,0:T(8,128)(4,1)S(1)} %copy-done.2), kind=kLoop, calls=%fused_computation.25 | loop fusion | flops 9435648 | bytes 9596928 | tf_op jit(solution)/shard_map/cond/branch_1_fun/reduce_sum | solution.py:55
  134.1 1.4 divide_bitcast_fusion
  135.5 0.5 copy.21
  136.0 0.3 bitcast_multiply_fusion
  136.2 0.0 copy-done
  136.3 1.3 fusion.28
  137.6 3.0 %psum.7 = f32[192]{0:T(256)} all-reduce(f32[192]{0:T(256)S(1)} %bitcast.94), channel_id=1, replica_groups=mesh['groups'=2,'ctx'=8,'tp'=2] {'tp'}, use_global_device_ids=true, to_apply=%region_8.9 | all-reduce | flops 192 | bytes 1536 | tf_op jit(solution)/shard_map/psum | solution.py:143
  140.6 1.0 fusion.29
  (16 shorter events, 0.1 us)
Async XLA Ops:
  0.6 135.6 %copy-start = (f32[2048]{0:T(1024)S(1)}, f32[2048]{0:T(1024)}, u32[]{:S(2)}) copy-start(f32[2048]{0:T(1024)} %param.15) | copy-start | bytes 24580
  0.6 25.0 %copy-start.4 = (bf16[192,256]{1,0:T(8,128)(2,1)S(1)}, bf16[192,256]{1,0:T(8,128)(2,1)}, u32[]{:S(2)}) copy-start(bf16[192,256]{1,0:T(8,128)(2,1)} %param.11) | copy-start | bytes 294916
  0.7 58.4 %copy-start.3 = (bf16[192,256]{1,0:T(8,128)(2,1)S(1)}, bf16[192,256]{1,0:T(8,128)(2,1)}, u32[]{:S(2)}) copy-start(bf16[192,256]{1,0:T(8,128)(2,1)} %param.12) | copy-start | bytes 294916
  100.0 7.6 %slice-start = ((s8[9437184]{0:T(1024)(128)(4,1)}), s8[1048576]{0:T(1024)(128)(4,1)S(1)}, s32[]{:S(2)}) async-start(s8[9437184]{0:T(1024)(128)(4,1)} %bitcast.76), calls=%async_computation | async-start | bytes 2097152 | tf_op jit(solution)/shard_map/cond
  101.1 6.6 %slice-start.1 = ((s8[9437184]{0:T(1024)(128)(4,1)}), s8[4194304]{0:T(1024)(128)(4,1)S(1)}, s32[]{:S(2)}) async-start(s8[9437184]{0:T(1024)(128)(4,1)} %bitcast.76), calls=%async_computation.1 | async-start | bytes 8388608 | tf_op jit(solution)/shard_map/cond
  101.1 6.6 %slice-start.2 = ((s8[9437184]{0:T(1024)(128)(4,1)}), s8[4194304]{0:T(1024)(128)(4,1)S(1)}, s32[]{:S(2)}) async-start(s8[9437184]{0:T(1024)(128)(4,1)} %bitcast.76), calls=%async_computation.2 | async-start | bytes 8388608 | tf_op jit(solution)/shard_map/cond
  115.5 2.1 %copy-start.1 = (pred[96,1536]{1,0:T(8,128)(4,1)}, pred[96,1536]{1,0:T(8,128)(4,1)S(1)}, u32[]{:S(2)}) copy-start(pred[96,1536]{1,0:T(8,128)(4,1)S(1)} %or_and_fusion.1) | copy-start | bytes 442372 | tf_op jit(solution)/shard_map/cond
  123.9 7.7 %slice-start.3 = ((s8[9437184]{0:T(1024)(128)(4,1)}), s8[1048576]{0:T(1024)(128)(4,1)S(1)}, s32[]{:S(2)}) async-start(s8[9437184]{0:T(1024)(128)(4,1)} %bitcast.78), calls=%async_computation.3 | async-start | bytes 2097152 | tf_op jit(solution)/shard_map/cond
  123.9 7.7 %copy-start.2 = (pred[96,1536]{1,0:T(8,128)(4,1)S(1)}, pred[96,1536]{1,0:T(8,128)(4,1)}, u32[]{:S(2)}) copy-start(pred[96,1536]{1,0:T(8,128)(4,1)} %copy-done.1) | copy-start | bytes 442372 | tf_op jit(solution)/shard_map/cond
  124.9 6.6 %slice-start.4 = ((s8[9437184]{0:T(1024)(128)(4,1)}), s8[4194304]{0:T(1024)(128)(4,1)S(1)}, s32[]{:S(2)}) async-start(s8[9437184]{0:T(1024)(128)(4,1)} %bitcast.78), calls=%async_computation.4 | async-start | bytes 8388608 | tf_op jit(solution)/shard_map/cond
  124.9 6.6 %slice-start.5 = ((s8[9437184]{0:T(1024)(128)(4,1)}), s8[4194304]{0:T(1024)(128)(4,1)S(1)}, s32[]{:S(2)}) async-start(s8[9437184]{0:T(1024)(128)(4,1)} %bitcast.78), calls=%async_computation.5 | async-start | bytes 8388608 | tf_op jit(solution)/shard_map/cond
where the time goes:
time: 142 us
  blocking collectives  80.4 us (57%)
  matrix products  26.1 us (18%)
  other arithmetic  14.8 us (10%)
  local copies, waits for them, and re-layouts  11.4 us (8%)
  between operations  8.48 us (6%)
    all_gather x1, blocking collectives, per_device(): key_rows = lax.all_gather(k_rot, 'ctx', axis=0, tiled=True)  32.5 us
    all_gather x1, blocking collectives, per_device(): value_rows = lax.all_gather(values, 'ctx', axis=0, tiled=True)  31.7 us
    unnamed x1, blocking collectives  13.2 us
    dot_general x2, matrix products, attend(): jnp.einsum('kgrs,skd->kgrd', weights.astype(jnp.bfloat16), value_three, p...  13.2 us
    dot_general x2, matrix products, attend(): jnp.einsum('rkgd,skd->kgrs', query_four, key_three, preferred_element_typ...  11.6 us
    reduce_sum x2, other arithmetic, attend(): new_sum = jnp.sum(weights, axis=-1)  4.94 us
    unnamed x12, local copies, waits for them, and re-layouts  3.54 us
    psum x1, blocking collectives, per_device(): reward = lax.psum(partial_reward, 'tp')  3.02 us

commit v1 on v0

v1 whole, which is shorter than its diff:
```python
import functools
import math

import jax
import jax.numpy as jnp
from jax import lax
from jax.experimental import pallas as pl
from jax.experimental.pallas import tpu as pltpu
from jax.sharding import PartitionSpec as P

HEAD = 128
LANES = 128
MESH = pl.DeviceIdType.MESH
SCALE = HEAD**-0.5 * math.log2(math.e)
BLOCKED = -1e30


def kernel(
    n,
    window,
    ways,
    q_hbm,
    k_ref,
    v_ref,
    seg_ref,
    valid_ref,
    weight_ref,
    out_hbm,
    reward_ref,
    q_in,
    q_rot,
    k_own,
    k_buf,
    v_buf,
    seg_own,
    seg_buf,
    bias_ref,
    max_ref,
    acc_ref,
    out_buf,
    rew_acc,
    rew_own,
    rew_far,
    send_sem,
    recv_sem,
    local_sem,
    rew_sem,
):
    rows = k_ref.shape[0]
    kv_heads = k_ref.shape[1] // HEAD
    q_heads = q_in.shape[1] // HEAD
    group = q_heads // kv_heads
    chunks = 1 + 2 * kv_heads
    me = lax.axis_index("ctx")
    other = 1 - lax.axis_index("tp")
    odd = lax.rem(me, 2)

    load = pltpu.make_async_copy(q_hbm, q_in, local_sem.at[0])
    load.start()

    def outgoing(slot):
        held = me - 1 - slot >= 0
        if ways == 1:
            return [(0, slot + 1, me + 1, held & (me + 1 < n))] if slot + 1 < window else []
        sends = []
        if slot == -1 or slot % 2 == 1:
            if slot + 2 < window:
                sends.append((0, slot + 2, me + 2, held & (me + 2 < n)))
            if slot + 1 < window:
                sends.append((1, slot + 1, me + 1, held & (odd == 0)))
            if slot >= 1:
                sends.append((2, slot - 1, me - 1, held & (odd == 1)))
        return sends

    def piece(slot, chunk):
        if chunk == 0:
            return seg_own if slot < 0 else seg_buf.at[slot]
        head, is_key = (chunk - 1) // 2, (chunk - 1) % 2 == 1
        if slot < 0:
            return k_own.at[head] if is_key else v_ref.at[:, pl.ds(head * HEAD, HEAD)]
        return (k_buf if is_key else v_buf).at[head, pl.ds(slot * rows, rows)]

    def copy_of(slot, chunk, path, there, device):
        return pltpu.make_async_remote_copy(
            src_ref=piece(slot, chunk),
            dst_ref=piece(there, chunk),
            send_sem=send_sem.at[path, there, chunk],
            recv_sem=recv_sem.at[there, chunk],
            device_id={"ctx": device},
            device_id_type=MESH,
        )

    def send(slot, chunk):
        for path, there, device, condition in outgoing(slot):
            @pl.when(condition)
            def _(path=path, there=there, device=device):
                copy_of(slot, chunk, path, there, device).start()

    def finish_send(slot, chunk):
        for path, there, device, condition in outgoing(slot):
            @pl.when(condition)
            def _(path=path, there=there, device=device):
                copy_of(slot, chunk, path, there, device).wait_send()

    def arrive(slot, chunk):
        @pl.when(me - 1 - slot >= 0)
        def _():
            copy_of(slot, chunk, 0, slot, me).wait_recv()

        send(slot, chunk)

    seg_own[...] = jnp.zeros_like(seg_own)
    seg_own[:, :rows] = seg_ref[...]
    for slot in range(window):
        @pl.when(me - 1 - slot < 0)
        def _(slot=slot):
            seg_buf[slot] = jnp.zeros(seg_buf.shape[1:], seg_buf.dtype)
            for head in range(kv_heads):
                k_buf[head, slot * rows : (slot + 1) * rows] = jnp.zeros((rows, HEAD), k_buf.dtype)
                v_buf[head, slot * rows : (slot + 1) * rows] = jnp.zeros((rows, HEAD), v_buf.dtype)

    barrier = pltpu.get_barrier_semaphore()
    pl.semaphore_signal(barrier, inc=1, device_id={"tp": other}, device_id_type=MESH)
    if ways == 2:
        pl.semaphore_signal(barrier, inc=1, device_id={"ctx": me + 1 - 2 * odd}, device_id_type=MESH)

    @pl.when(me + ways < n)
    def _():
        pl.semaphore_signal(barrier, inc=1, device_id={"ctx": me + ways}, device_id_type=MESH)

    @pl.when(me >= ways)
    def _():
        pl.semaphore_signal(barrier, inc=1, device_id={"ctx": me - ways}, device_id_type=MESH)

    pl.semaphore_wait(
        barrier, ways + (me + ways < n).astype(jnp.int32) + (me >= ways).astype(jnp.int32)
    )

    send(-1, 0)
    for head in range(kv_heads):
        send(-1, 1 + 2 * head)

    lane = lax.broadcasted_iota(jnp.int32, (1, HEAD), 1)
    step = lax.rem(lane, HEAD // 2).astype(jnp.float32)
    frequency = jnp.exp(step * (-2.0 * math.log(1000000.0) / HEAD))
    position = me * rows + lax.broadcasted_iota(jnp.int32, (rows, 1), 0)
    angles = position.astype(jnp.float32) * frequency
    cosine = jnp.cos(angles)
    sine = jnp.where(lane < HEAD // 2, -1.0, 1.0) * jnp.sin(angles)

    def rotated(entries):
        wide = entries.astype(jnp.float32)
        return (wide * cosine + pltpu.roll(wide, HEAD // 2, 1) * sine).astype(jnp.bfloat16)

    for head in range(kv_heads):
        k_own[head] = rotated(k_ref[:, head * HEAD : (head + 1) * HEAD])
        send(-1, 2 + 2 * head)
    load.wait()
    for head in range(q_heads):
        q_rot[head] = rotated(q_in[:, head * HEAD : (head + 1) * HEAD])

    valid = valid_ref[0]
    row_at = lax.broadcasted_iota(jnp.int32, (rows, rows), 0)
    col_at = lax.broadcasted_iota(jnp.int32, (rows, rows), 1)
    seg_row = seg_ref[...]
    seg_col = jnp.sum(jnp.where(row_at == col_at, seg_row, 0), axis=1, keepdims=True)
    ones = jnp.ones((2 * rows, HEAD), jnp.bfloat16)

    def scores_of(head, keys, bias):
        s = lax.dot_general(
            q_rot[head], keys, (((1,), (1,)), ((), ())), preferred_element_type=jnp.float32
        )
        return s * SCALE + bias

    causal = (seg_row == seg_col) & (col_at <= row_at)
    causal = causal & ((me * rows + col_at < valid) | (col_at == row_at))
    bias_ref[:, :rows] = jnp.where(causal, 0.0, BLOCKED)
    per_step = min(4, group)

    def first(head):
        kv = head // group
        t = scores_of(head, k_own[kv], bias_ref[:, :rows])
        top = jnp.max(t, axis=1, keepdims=True)
        p = jnp.exp2(t - top).astype(jnp.bfloat16)
        v = jnp.concatenate([v_ref[:, kv * HEAD : (kv + 1) * HEAD], ones[:rows]], axis=1)
        acc_ref[head] = jnp.dot(p, v, preferred_element_type=jnp.float32)
        max_ref[head] = jnp.broadcast_to(top, (rows, LANES))

    for head in range(q_heads):
        first(head)

    def later(stage, kv, last):
        span = pl.ds(2 * stage * rows, 2 * rows)

        def body(step, carry):
            for inner in range(per_step):
                head = kv * group + step * per_step + inner
                t = scores_of(head, k_buf[kv, span], bias_ref[...])
                before = max_ref[head]
                top = jnp.maximum(jnp.max(t, axis=1, keepdims=True), before[:, :1])
                p = jnp.exp2(t - top).astype(jnp.bfloat16)
                v = jnp.concatenate([v_buf[kv, span], ones], axis=1)
                mixed = jnp.dot(p, v, preferred_element_type=jnp.float32)
                total = acc_ref[head] * jnp.exp2(before[:, :1] - top) + mixed
                if last:
                    out = total[:, :HEAD] / total[:, HEAD:]
                    out = jnp.where(position < valid, out, 0.0)
                    rew_acc[...] += out * weight_ref[pl.ds(head, 1), :]
                    columns = pl.ds(pl.multiple_of(head * HEAD, HEAD), HEAD)
                    out_buf[:, columns] = out.astype(jnp.bfloat16)
                else:
                    acc_ref[head] = total
                    max_ref[head] = jnp.broadcast_to(top, (rows, LANES))
            return carry

        lax.fori_loop(0, group // per_step, body, 0)

    rew_acc[...] = jnp.zeros_like(rew_acc)
    stages = window // 2
    lane_at = lax.broadcasted_iota(jnp.int32, (1, 2 * rows), 1)
    second = (lane_at >= rows).astype(jnp.int32)
    stores = []
    for stage in range(stages):
        near, far = 2 * stage, 2 * stage + 1
        order = (far, near) if ways == 2 else (near, far)
        for slot in order:
            arrive(slot, 0)
        seg_keys = jnp.concatenate([seg_buf[near][:, :rows], seg_buf[far][:, :rows]], axis=1)
        key_pos = (me - 1 - near - second) * rows + lane_at - second * rows
        allowed = (seg_keys == seg_col) & (key_pos >= 0) & (key_pos < valid)
        bias_ref[...] = jnp.where(allowed, 0.0, BLOCKED)
        last = stage == stages - 1
        if not last:
            for slot in order:
                for chunk in range(1, chunks):
                    arrive(slot, chunk)
        for kv in range(kv_heads):
            if last:
                for slot in order:
                    arrive(slot, 1 + 2 * kv)
                    arrive(slot, 2 + 2 * kv)
                if ways == 2 and kv == 0 and kv_heads > 1:
                    pass
            later(stage, kv, last)
            if last:
                columns = pl.ds(kv * group * HEAD, group * HEAD)
                store = pltpu.make_async_copy(
                    out_buf.at[:, columns], out_hbm.at[:, columns], local_sem.at[1 + kv]
                )
                store.start()
                stores.append(store)

    mine = jnp.sum(rew_acc[...], axis=1, keepdims=True)
    mine_row = jnp.sum(jnp.where(row_at == col_at, mine, 0.0), axis=0, keepdims=True)
    rew_own[...] = jnp.zeros_like(rew_own)
    rew_own[:, :rows] = mine_row
    swap = pltpu.make_async_remote_copy(
        src_ref=rew_own,
        dst_ref=rew_far,
        send_sem=rew_sem.at[0],
        recv_sem=rew_sem.at[1],
        device_id={"tp": other},
        device_id_type=MESH,
    )
    swap.start()
    for slot in range(-1, window):
        for chunk in range(chunks):
            finish_send(slot, chunk)
    swap.wait()
    reward_ref[...] = mine_row + rew_far[:, :rows]
    for store in stores:
        store.wait()


def per_device(n, queries, keys, values, segments, valid_length, reward_weight):
    rows = queries.shape[0]
    q_heads = queries.shape[1] // HEAD
    kv_heads = keys.shape[1] // HEAD
    span = rows * n // 2
    window = -(-(span - 1) // rows)
    window += window % 2
    ways = 2 if n <= 8 else 1
    chunks = 1 + 2 * kv_heads
    wide = -(-rows // LANES) * LANES
    vmem = pl.BlockSpec(memory_space=pltpu.VMEM)
    attention, reward = pl.pallas_call(
        functools.partial(kernel, n, window, ways),
        out_shape=(
            jax.ShapeDtypeStruct(queries.shape, jnp.bfloat16),
            jax.ShapeDtypeStruct((1, rows), jnp.float32),
        ),
        in_specs=[
            pl.BlockSpec(memory_space=pl.ANY),
            vmem,
            vmem,
            vmem,
            pl.BlockSpec(memory_space=pltpu.SMEM),
            vmem,
        ],
        out_specs=(pl.BlockSpec(memory_space=pl.ANY), vmem),
        scratch_shapes=[
            pltpu.VMEM(queries.shape, jnp.bfloat16),
            pltpu.VMEM((q_heads, rows, HEAD), jnp.bfloat16),
            pltpu.VMEM((kv_heads, rows, HEAD), jnp.bfloat16),
            pltpu.VMEM((kv_heads, window * rows, HEAD), jnp.bfloat16),
            pltpu.VMEM((kv_heads, window * rows, HEAD), jnp.bfloat16),
            pltpu.VMEM((1, wide), jnp.int32),
            pltpu.VMEM((window, 1, wide), jnp.int32),
            pltpu.VMEM((rows, 2 * rows), jnp.float32),
            pltpu.VMEM((q_heads, rows, LANES), jnp.float32),
            pltpu.VMEM((q_heads, rows, 2 * HEAD), jnp.float32),
            pltpu.VMEM(queries.shape, jnp.bfloat16),
            pltpu.VMEM((rows, HEAD), jnp.float32),
            pltpu.VMEM((1, wide), jnp.float32),
            pltpu.VMEM((1, wide), jnp.float32),
            pltpu.SemaphoreType.DMA((3, window, chunks)),
            pltpu.SemaphoreType.DMA((window, chunks)),
            pltpu.SemaphoreType.DMA((1 + kv_heads,)),
            pltpu.SemaphoreType.DMA((2,)),
        ],
        compiler_params=pltpu.CompilerParams(
            collective_id=0, has_side_effects=True, vmem_limit_bytes=48 * 1024 * 1024
        ),
    )(
        queries,
        keys,
        values,
        segments.reshape(1, rows),
        valid_length,
        reward_weight.reshape(q_heads, HEAD),
    )
    return attention, reward.reshape(rows)


def solution(mesh):
    return jax.shard_map(
        functools.partial(per_device, mesh.shape["ctx"]),
        mesh=mesh,
        in_specs=(
            P(("groups", "ctx"), "tp"),
            P(("groups", "ctx"), "tp"),
            P(("groups", "ctx"), "tp"),
            P(("groups", "ctx")),
            P("groups"),
            P("tp"),
        ),
        out_specs=(P(("groups", "ctx"), "tp"), P(("groups", "ctx"))),
        check_vma=False,
    )
```

time: 142 us -> 32 us (0.23)
  the two profiles are of different devices: /device:TPU:0 before, /device:TPU:17 now
where the time goes in v1:
time: 32 us; the launch traced here: 31.6 us
  Pallas kernels  24.6 us (77%)
  local copies, waits for them, and re-layouts  5.73 us (18%)
  between operations  1.3 us (4%)
    pallas_call x1, Pallas kernels, per_device(): pl.pallas_call(functools.partial(kernel, n, window, ways), out_shape=(jax...  24.6 us
    unnamed x12, local copies, waits for them, and re-layouts  5.73 us

profile of v1, /device:TPU:17, one launch (start us, length us, event | category | flops | bytes accessed | tf_op | source)
XLA Modules:
  0.0 31.6 jit_solution(5557000749409051407)
XLA Ops:
  1.3 0.0 copy-start.4
  1.3 0.7 %copy-done.4 = s32[192]{0:T(256)S(1)} copy-done((s32[192]{0:T(256)S(1)}, s32[192]{0:T(256)}, u32[]{:S(2)}) %copy-start.4) | copy-done | bytes 792
  2.0 0.0 copy-start
  2.0 1.1 %copy-done = bf16[192,2048]{1,0:T(8,128)(2,1)S(1)} copy-done((bf16[192,2048]{1,0:T(8,128)(2,1)S(1)}, bf16[192,2048]{1,0:T(8,128)(2,1)}, u32[]{:S(2)}) %copy-start) | copy-done | bytes 786456
  3.1 0.0 copy-start.1
  3.1 0.9 %copy-done.1 = bf16[192,256]{1,0:T(8,128)(2,1)S(1)} copy-done((bf16[192,256]{1,0:T(8,128)(2,1)S(1)}, bf16[192,256]{1,0:T(8,128)(2,1)}, u32[]{:S(2)}) %copy-start.1) | copy-done | bytes 98328
  4.0 0.0 copy-start.2
  4.0 0.9 %copy-done.2 = bf16[192,256]{1,0:T(8,128)(2,1)S(1)} copy-done((bf16[192,256]{1,0:T(8,128)(2,1)S(1)}, bf16[192,256]{1,0:T(8,128)(2,1)}, u32[]{:S(2)}) %copy-start.2) | copy-done | bytes 98328
  4.9 0.0 copy-start.3
  4.9 0.7 %copy-done.3 = f32[2048]{0:T(1024)S(1)} copy-done((f32[2048]{0:T(1024)S(1)}, f32[2048]{0:T(1024)}, u32[]{:S(2)}) %copy-start.3) | copy-done | bytes 8216
  5.6 24.6 %shard_map.77 = (bf16[192,2048]{1,0:T(8,128)(2,1)S(1)}, f32[1,192]{1,0:T(1,128)S(1)}) custom-call(bf16[192,2048]{1,0:T(8,128)(2,1)S(1)} %copy-done, bf16[192,256]{1,0:T(8,128)(2,1)S(1)} %copy-done.1, bf16[192,256]{1,0:T(8,128)(2,1)S(1)} %copy-done.2, s32[1,192]{1,0:T(1,128)S(1)} %bitcast.5, s32[1]{0:T(128)S(6)} %copy.10.valid_ref, f32[16,128]{1,0:T(8,128)S(1)} %bitcast.3), custom_call_target="tpu_custom_call" | custom-call | tf_op jit(solution)/shard_map/pallas_call | solution.py:286
  30.2 0.9 %copy.11 = bf16[192,2048]{1,0:T(8,128)(2,1)} copy(bf16[192,2048]{1,0:T(8,128)(2,1)S(1)} %get-tuple-element.8) | data formatting | bytes 1572864
  31.0 0.6 %copy.12 = f32[192]{0:T(256)} copy(f32[192]{0:T(256)S(1)} %bitcast.4) | data formatting | bytes 1536
Async XLA Ops:
  1.3 0.7 %copy-start.4 = (s32[192]{0:T(256)S(1)}, s32[192]{0:T(256)}, u32[]{:S(2)}) copy-start(s32[192]{0:T(256)} %param.9) | copy-start | bytes 2308
  2.0 1.1 %copy-start = (bf16[192,2048]{1,0:T(8,128)(2,1)S(1)}, bf16[192,2048]{1,0:T(8,128)(2,1)}, u32[]{:S(2)}) copy-start(bf16[192,2048]{1,0:T(8,128)(2,1)} %q_hbm.1) | copy-start | bytes 2359300
  3.1 0.9 %copy-start.1 = (bf16[192,256]{1,0:T(8,128)(2,1)S(1)}, bf16[192,256]{1,0:T(8,128)(2,1)}, u32[]{:S(2)}) copy-start(bf16[192,256]{1,0:T(8,128)(2,1)} %k_ref.1) | copy-start | bytes 294916
  4.0 0.9 %copy-start.2 = (bf16[192,256]{1,0:T(8,128)(2,1)S(1)}, bf16[192,256]{1,0:T(8,128)(2,1)}, u32[]{:S(2)}) copy-start(bf16[192,256]{1,0:T(8,128)(2,1)} %v_ref.1) | copy-start | bytes 294916
  4.9 0.7 %copy-start.3 = (f32[2048]{0:T(1024)S(1)}, f32[2048]{0:T(1024)}, u32[]{:S(2)}) copy-start(f32[2048]{0:T(1024)} %param.11) | copy-start | bytes 24580

commit v2 on v1

--- a/solution.py
+++ b/solution.py
@@ -20,14 +20,18 @@
     window,
     ways,
     q_hbm,
+    k_hbm,
+    v_hbm,
+    seg_hbm,
+    valid_ref,
+    weight_hbm,
+    out_hbm,
+    reward_ref,
+    q_in,
     k_ref,
     v_ref,
     seg_ref,
-    valid_ref,
     weight_ref,
-    out_hbm,
-    reward_ref,
-    q_in,
     q_rot,
     k_own,
     k_buf,
@@ -45,6 +49,7 @@
     recv_sem,
     local_sem,
     rew_sem,
+    load_sem,
 ):
     rows = k_ref.shape[0]
     kv_heads = k_ref.shape[1] // HEAD
@@ -55,8 +60,24 @@
     other = 1 - lax.axis_index("tp")
     odd = lax.rem(me, 2)
 
-    load = pltpu.make_async_copy(q_hbm, q_in, local_sem.at[0])
-    load.start()
+    barrier = pltpu.get_barrier_semaphore()
+    pl.semaphore_signal(barrier, inc=1, device_id={"tp": other}, device_id_type=MESH)
+    if ways == 2:
+        pl.semaphore_signal(barrier, inc=1, device_id={"ctx": me + 1 - 2 * odd}, device_id_type=MESH)
+
+    @pl.when(me + ways < n)
+    def _():
+        pl.semaphore_signal(barrier, inc=1, device_id={"ctx": me + ways}, device_id_type=MESH)
+
+    @pl.when(me >= ways)
+    def _():
+        pl.semaphore_signal(barrier, inc=1, device_id={"ctx": me - ways}, device_id_type=MESH)
+
+    loads = []
+    pairs = ((v_hbm, v_ref), (seg_hbm, seg_ref), (k_hbm, k_ref), (q_hbm, q_in), (weight_hbm, weight_ref))
+    for at, (source, target) in enumerate(pairs):
+        loads.append(pltpu.make_async_copy(source, target, load_sem.at[at]))
+        loads[-1].start()
 
     def outgoing(slot):
         held = me - 1 - slot >= 0
@@ -109,8 +130,6 @@
 
         send(slot, chunk)
 
-    seg_own[...] = jnp.zeros_like(seg_own)
-    seg_own[:, :rows] = seg_ref[...]
     for slot in range(window):
         @pl.when(me - 1 - slot < 0)
         def _(slot=slot):
@@ -119,19 +138,10 @@
                 k_buf[head, slot * rows : (slot + 1) * rows] = jnp.zeros((rows, HEAD), k_buf.dtype)
                 v_buf[head, slot * rows : (slot + 1) * rows] = jnp.zeros((rows, HEAD), v_buf.dtype)
 
-    barrier = pltpu.get_barrier_semaphore()
-    pl.semaphore_signal(barrier, inc=1, device_id={"tp": other}, device_id_type=MESH)
-    if ways == 2:
-        pl.semaphore_signal(barrier, inc=1, device_id={"ctx": me + 1 - 2 * odd}, device_id_type=MESH)
-
-    @pl.when(me + ways < n)
-    def _():
-        pl.semaphore_signal(barrier, inc=1, device_id={"ctx": me + ways}, device_id_type=MESH)
-
-    @pl.when(me >= ways)
-    def _():
-        pl.semaphore_signal(barrier, inc=1, device_id={"ctx": me - ways}, device_id_type=MESH)
-
+    loads[1].wait()
+    seg_own[...] = jnp.zeros_like(seg_own)
+    seg_own[:, :rows] = seg_ref[...]
+    loads[0].wait()
     pl.semaphore_wait(
         barrier, ways + (me + ways < n).astype(jnp.int32) + (me >= ways).astype(jnp.int32)
     )
@@ -152,10 +162,11 @@
         wide = entries.astype(jnp.float32)
         return (wide * cosine + pltpu.roll(wide, HEAD // 2, 1) * sine).astype(jnp.bfloat16)
 
+    loads[2].wait()
     for head in range(kv_heads):
         k_own[head] = rotated(k_ref[:, head * HEAD : (head + 1) * HEAD])
         send(-1, 2 + 2 * head)
-    load.wait()
+    loads[3].wait()
     for head in range(q_heads):
         q_rot[head] = rotated(q_in[:, head * HEAD : (head + 1) * HEAD])
 
@@ -215,6 +226,7 @@
 
         lax.fori_loop(0, group // per_step, body, 0)
 
+    loads[4].wait()
     rew_acc[...] = jnp.zeros_like(rew_acc)
     stages = window // 2
     lane_at = lax.broadcasted_iota(jnp.int32, (1, 2 * rows), 1)
@@ -239,8 +251,6 @@
                 for slot in order:
                     arrive(slot, 1 + 2 * kv)
                     arrive(slot, 2 + 2 * kv)
-                if ways == 2 and kv == 0 and kv_heads > 1:
-                    pass
             later(stage, kv, last)
             if last:
                 columns = pl.ds(kv * group * HEAD, group * HEAD)
@@ -283,6 +293,7 @@
     chunks = 1 + 2 * kv_heads
     wide = -(-rows // LANES) * LANES
     vmem = pl.BlockSpec(memory_space=pltpu.VMEM)
+    hbm = pl.BlockSpec(memory_space=pl.ANY)
     attention, reward = pl.pallas_call(
         functools.partial(kernel, n, window, ways),
         out_shape=(
@@ -290,16 +301,20 @@
             jax.ShapeDtypeStruct((1, rows), jnp.float32),
         ),
         in_specs=[
-            pl.BlockSpec(memory_space=pl.ANY),
-            vmem,
-            vmem,
-            vmem,
+            hbm,
+            hbm,
+            hbm,
+            hbm,
             pl.BlockSpec(memory_space=pltpu.SMEM),
-            vmem,
+            hbm,
         ],
-        out_specs=(pl.BlockSpec(memory_space=pl.ANY), vmem),
+        out_specs=(hbm, vmem),
         scratch_shapes=[
             pltpu.VMEM(queries.shape, jnp.bfloat16),
+            pltpu.VMEM(keys.shape, jnp.bfloat16),
+            pltpu.VMEM(values.shape, jnp.bfloat16),
+            pltpu.VMEM((1, rows), jnp.int32),
+            pltpu.VMEM((q_heads, HEAD), jnp.float32),
             pltpu.VMEM((q_heads, rows, HEAD), jnp.bfloat16),
             pltpu.VMEM((kv_heads, rows, HEAD), jnp.bfloat16),
             pltpu.VMEM((kv_heads, window * rows, HEAD), jnp.bfloat16),
@@ -317,9 +332,10 @@
             pltpu.SemaphoreType.DMA((window, chunks)),
             pltpu.SemaphoreType.DMA((1 + kv_heads,)),
             pltpu.SemaphoreType.DMA((2,)),
+            pltpu.SemaphoreType.DMA((5,)),
         ],
         compiler_params=pltpu.CompilerParams(
-            collective_id=0, has_side_effects=True, vmem_limit_bytes=48 * 1024 * 1024
+            collective_id=0, has_side_effects=True, vmem_limit_bytes=60 * 1024 * 1024
         ),
     )(
         queries,

time: 32 us -> 29 us (0.906)
  local copies, waits for them, and re-layouts: 5.73 us -> 2.66 us
    unnamed x12 -> x4, local copies, waits for them, and re-layouts: 5.73 us -> 2.66 us
where the time goes in v2:
time: 29 us; the launch traced here: 28.8 us
  Pallas kernels  24.9 us (86%)
  local copies, waits for them, and re-layouts  2.66 us (9%)
  between operations  1.29 us (4%)
    pallas_call x1, Pallas kernels, per_device(): pl.pallas_call(functools.partial(kernel, n, window, ways), out_shape=(jax...  24.9 us
    unnamed x4, local copies, waits for them, and re-layouts  2.66 us

profile of v2, /device:TPU:17, one launch (start us, length us, event | category | flops | bytes accessed | tf_op | source)
XLA Modules:
  0.0 28.8 jit_solution(802307300641454733)
XLA Ops:
  1.3 24.9 %shard_map.77 = (bf16[192,2048]{1,0:T(8,128)(2,1)}, f32[1,192]{1,0:T(1,128)}) custom-call(bf16[192,2048]{1,0:T(8,128)(2,1)} %q_hbm.1, bf16[192,256]{1,0:T(8,128)(2,1)} %k_hbm.1, bf16[192,256]{1,0:T(8,128)(2,1)} %v_hbm.1, s32[1,192]{1,0:T(1,128)} %bitcast.5, s32[1]{0:T(128)S(6)} %copy.10.valid_ref, f32[16,128]{1,0:T(8,128)} %bitcast.3), custom_call_target="tpu_custom_call" | custom-call | tf_op jit(solution)/shard_map/pallas_call | solution.py:297
  26.2 0.0 copy-start
  26.2 2.1 %copy.11 = bf16[192,2048]{1,0:T(8,128)(2,1)} copy(bf16[192,2048]{1,0:T(8,128)(2,1)} %get-tuple-element.8) | data formatting | bytes 1572864
  28.3 0.0 copy-done
  28.3 0.6 %copy.12 = f32[192]{0:T(256)} copy(f32[192]{0:T(256)S(1)} %bitcast.4) | data formatting | bytes 1536
Async XLA Ops:
  26.2 2.1 %copy-start = (f32[1,192]{1,0:T(1,128)S(1)}, f32[1,192]{1,0:T(1,128)}, u32[]{:S(2)}) copy-start(f32[1,192]{1,0:T(1,128)} %get-tuple-element.5) | copy-start | bytes 2308

commit v3 on v2

--- a/solution.py
+++ b/solution.py
@@ -13,6 +13,8 @@
 MESH = pl.DeviceIdType.MESH
 SCALE = HEAD**-0.5 * math.log2(math.e)
 BLOCKED = -1e30
+BATCH = 4
+PART = 96
 
 
 def kernel(
@@ -23,15 +25,16 @@
     k_hbm,
     v_hbm,
     seg_hbm,
-    valid_ref,
+    valid_hbm,
     weight_hbm,
-    out_hbm,
+    out_buf,
     reward_ref,
     q_in,
     k_ref,
     v_ref,
     seg_ref,
     weight_ref,
+    valid_ref,
     q_rot,
     k_own,
     k_buf,
@@ -41,13 +44,11 @@
     bias_ref,
     max_ref,
     acc_ref,
-    out_buf,
     rew_acc,
     rew_own,
     rew_far,
     send_sem,
     recv_sem,
-    local_sem,
     rew_sem,
     load_sem,
 ):
@@ -74,7 +75,7 @@
         pl.semaphore_signal(barrier, inc=1, device_id={"ctx": me - ways}, device_id_type=MESH)
 
     loads = []
-    pairs = ((v_hbm, v_ref), (seg_hbm, seg_ref), (k_hbm, k_ref), (q_hbm, q_in), (weight_hbm, weight_ref))
+    pairs = ((v_hbm, v_ref), (seg_hbm, seg_ref), (k_hbm, k_ref), (q_hbm, q_in), (weight_hbm, weight_ref), (valid_hbm, valid_ref))
     for at, (source, target) in enumerate(pairs):
         loads.append(pltpu.make_async_copy(source, target, load_sem.at[at]))
         loads[-1].start()
@@ -123,7 +124,13 @@
             def _(path=path, there=there, device=device):
                 copy_of(slot, chunk, path, there, device).wait_send()
 
+    arrived = set()
+
     def arrive(slot, chunk):
+        if slot >= window or chunk >= chunks or (slot, chunk) in arrived:
+            return
+        arrived.add((slot, chunk))
+
         @pl.when(me - 1 - slot >= 0)
         def _():
             copy_of(slot, chunk, 0, slot, me).wait_recv()
@@ -141,15 +148,6 @@
     loads[1].wait()
     seg_own[...] = jnp.zeros_like(seg_own)
     seg_own[:, :rows] = seg_ref[...]
-    loads[0].wait()
-    pl.semaphore_wait(
-        barrier, ways + (me + ways < n).astype(jnp.int32) + (me >= ways).astype(jnp.int32)
-    )
-
-    send(-1, 0)
-    for head in range(kv_heads):
-        send(-1, 1 + 2 * head)
-
     lane = lax.broadcasted_iota(jnp.int32, (1, HEAD), 1)
     step = lax.rem(lane, HEAD // 2).astype(jnp.float32)
     frequency = jnp.exp(step * (-2.0 * math.log(1000000.0) / HEAD))
@@ -165,11 +163,20 @@
     loads[2].wait()
     for head in range(kv_heads):
         k_own[head] = rotated(k_ref[:, head * HEAD : (head + 1) * HEAD])
-        send(-1, 2 + 2 * head)
+    loads[0].wait()
+
+    pl.semaphore_wait(
+        barrier, ways + (me + ways < n).astype(jnp.int32) + (me >= ways).astype(jnp.int32)
+    )
+
+    for chunk in range(chunks):
+        send(-1, chunk)
+
     loads[3].wait()
     for head in range(q_heads):
         q_rot[head] = rotated(q_in[:, head * HEAD : (head + 1) * HEAD])
 
+    loads[5].wait()
     valid = valid_ref[0]
     row_at = lax.broadcasted_iota(jnp.int32, (rows, rows), 0)
     col_at = lax.broadcasted_iota(jnp.int32, (rows, rows), 1)
@@ -177,61 +184,70 @@
     seg_col = jnp.sum(jnp.where(row_at == col_at, seg_row, 0), axis=1, keepdims=True)
     ones = jnp.ones((2 * rows, HEAD), jnp.bfloat16)
 
-    def scores_of(head, keys, bias):
-        s = lax.dot_general(
-            q_rot[head], keys, (((1,), (1,)), ((), ())), preferred_element_type=jnp.float32
-        )
-        return s * SCALE + bias
+    def attend(head0, count, keys, values, bias, before, total):
+        width = keys.shape[0]
+        tiles = -(-width // LANES)
+        held = jnp.concatenate([values, ones[:width]], axis=1)
+        results = []
+        for part in range(0, count, BATCH):
+            q = q_rot[pl.ds(head0 + part, BATCH)].reshape(BATCH * rows, HEAD)
+            s = lax.dot_general(
+                q, keys, (((1,), (1,)), ((), ())), preferred_element_type=jnp.float32
+            )
+            for i in range(BATCH):
+                for r in range(0, rows, PART):
+                    t = s[i * rows + r : i * rows + r + PART] * SCALE + bias[r : r + PART]
+                    top = jnp.broadcast_to(jnp.max(t, axis=1, keepdims=True), (PART, LANES))
+                    if before is not None:
+                        old = before[head0 + part + i, r : r + PART]
+                        top = jnp.maximum(top, old)
+                    wide = jnp.concatenate([top] * tiles, axis=1)[:, :width]
+                    p = jnp.exp2(t - wide).astype(jnp.bfloat16)
+                    mixed = jnp.dot(p, held, preferred_element_type=jnp.float32)
+                    if before is not None:
+                        alpha = jnp.exp2(old - top)
+                        mixed += total[head0 + part + i, r : r + PART] * jnp.concatenate([alpha, alpha], axis=1)
+                    results.append((part + i, r, top, mixed))
+        return results
 
     causal = (seg_row == seg_col) & (col_at <= row_at)
     causal = causal & ((me * rows + col_at < valid) | (col_at == row_at))
     bias_ref[:, :rows] = jnp.where(causal, 0.0, BLOCKED)
     per_step = min(4, group)
 
-    def first(head):
-        kv = head // group
-        t = scores_of(head, k_own[kv], bias_ref[:, :rows])
-        top = jnp.max(t, axis=1, keepdims=True)
-        p = jnp.exp2(t - top).astype(jnp.bfloat16)
-        v = jnp.concatenate([v_ref[:, kv * HEAD : (kv + 1) * HEAD], ones[:rows]], axis=1)
-        acc_ref[head] = jnp.dot(p, v, preferred_element_type=jnp.float32)
-        max_ref[head] = jnp.broadcast_to(top, (rows, LANES))
-
-    for head in range(q_heads):
-        first(head)
-
-    def later(stage, kv, last):
+    def keep(head0, results):
+        for i, r, top, mixed in results:
+            acc_ref[head0 + i, r : r + PART] = mixed
+            max_ref[head0 + i, r : r + PART] = top
+
+    lead = ways - 1
+    polls = [(0,), (1,), (2,), ()]
+    for kv in range(kv_heads):
+        for step in range(group // per_step):
+            here = kv * group + step * per_step
+            values = v_ref[:, kv * HEAD : (kv + 1) * HEAD]
+            keep(here, attend(here, per_step, k_own[kv], values, bias_ref[:, :rows], None, None))
+            for chunk in polls.pop(0) if polls else ():
+                arrive(lead, chunk)
+
+    def later(stage, kv, step, last):
         span = pl.ds(2 * stage * rows, 2 * rows)
-
-        def body(step, carry):
-            for inner in range(per_step):
-                head = kv * group + step * per_step + inner
-                t = scores_of(head, k_buf[kv, span], bias_ref[...])
-                before = max_ref[head]
-                top = jnp.maximum(jnp.max(t, axis=1, keepdims=True), before[:, :1])
-                p = jnp.exp2(t - top).astype(jnp.bfloat16)
-                v = jnp.concatenate([v_buf[kv, span], ones], axis=1)
-                mixed = jnp.dot(p, v, preferred_element_type=jnp.float32)
-                total = acc_ref[head] * jnp.exp2(before[:, :1] - top) + mixed
-                if last:
-                    out = total[:, :HEAD] / total[:, HEAD:]
-                    out = jnp.where(position < valid, out, 0.0)
-                    rew_acc[...] += out * weight_ref[pl.ds(head, 1), :]
-                    columns = pl.ds(pl.multiple_of(head * HEAD, HEAD), HEAD)
-                    out_buf[:, columns] = out.astype(jnp.bfloat16)
-                else:
-                    acc_ref[head] = total
-                    max_ref[head] = jnp.broadcast_to(top, (rows, LANES))
-            return carry
-
-        lax.fori_loop(0, group // per_step, body, 0)
+        head0 = kv * group + step * per_step
+        results = attend(head0, per_step, k_buf[kv, span], v_buf[kv, span], bias_ref[...], max_ref, acc_ref)
+        if not last:
+            keep(head0, results)
+            return
+        for i, r, top, mixed in results:
+            out = mixed[:, :HEAD] / mixed[:, HEAD:]
+            out = jnp.where(position[r : r + PART] < valid, out, 0.0)
+            rew_acc[r : r + PART] += out * weight_ref[pl.ds(head0 + i, 1), :]
+            out_buf[r : r + PART, pl.ds((head0 + i) * HEAD, HEAD)] = out.astype(jnp.bfloat16)
 
     loads[4].wait()
     rew_acc[...] = jnp.zeros_like(rew_acc)
     stages = window // 2
     lane_at = lax.broadcasted_iota(jnp.int32, (1, 2 * rows), 1)
     second = (lane_at >= rows).astype(jnp.int32)
-    stores = []
     for stage in range(stages):
         near, far = 2 * stage, 2 * stage + 1
         order = (far, near) if ways == 2 else (near, far)
@@ -242,23 +258,19 @@
         allowed = (seg_keys == seg_col) & (key_pos >= 0) & (key_pos < valid)
         bias_ref[...] = jnp.where(allowed, 0.0, BLOCKED)
         last = stage == stages - 1
-        if not last:
+        for kv in range(kv_heads):
             for slot in order:
-                for chunk in range(1, chunks):
-                    arrive(slot, chunk)
-        for kv in range(kv_heads):
-            if last:
-                for slot in order:
-                    arrive(slot, 1 + 2 * kv)
-                    arrive(slot, 2 + 2 * kv)
-            later(stage, kv, last)
-            if last:
-                columns = pl.ds(kv * group * HEAD, group * HEAD)
-                store = pltpu.make_async_copy(
-                    out_buf.at[:, columns], out_hbm.at[:, columns], local_sem.at[1 + kv]
-                )
-                store.start()
-                stores.append(store)
+                arrive(slot, 1 + 2 * kv)
+                arrive(slot, 2 + 2 * kv)
+            steps = group // per_step
+            for step in range(steps):
+                later(stage, kv, step, last)
+                ahead = 2 * stage + lead + (0 if kv + 1 < kv_heads else 2)
+                after = 1 + 2 * (kv + 1) if kv + 1 < kv_heads else 1
+                if ahead > 2 * stage + 1:
+                    arrive(ahead, 0)
+                if step < 2:
+                    arrive(ahead, after + step)
 
     mine = jnp.sum(rew_acc[...], axis=1, keepdims=True)
     mine_row = jnp.sum(jnp.where(row_at == col_at, mine, 0.0), axis=0, keepdims=True)
@@ -278,8 +290,6 @@
             finish_send(slot, chunk)
     swap.wait()
     reward_ref[...] = mine_row + rew_far[:, :rows]
-    for store in stores:
-        store.wait()
 
 
 def per_device(n, queries, keys, values, segments, valid_length, reward_weight):
@@ -293,7 +303,7 @@
     chunks = 1 + 2 * kv_heads
     wide = -(-rows // LANES) * LANES
     vmem = pl.BlockSpec(memory_space=pltpu.VMEM)
-    hbm = pl.BlockSpec(memory_space=pl.ANY)
+    hbm = pl.BlockSpec(memory_space=pltpu.HBM)
     attention, reward = pl.pallas_call(
         functools.partial(kernel, n, window, ways),
         out_shape=(
@@ -305,16 +315,17 @@
             hbm,
             hbm,
             hbm,
-            pl.BlockSpec(memory_space=pltpu.SMEM),
+            hbm,
             hbm,
         ],
-        out_specs=(hbm, vmem),
+        out_specs=(vmem, vmem),
         scratch_shapes=[
             pltpu.VMEM(queries.shape, jnp.bfloat16),
             pltpu.VMEM(keys.shape, jnp.bfloat16),
             pltpu.VMEM(values.shape, jnp.bfloat16),
             pltpu.VMEM((1, rows), jnp.int32),
             pltpu.VMEM((q_heads, HEAD), jnp.float32),
+            pltpu.SMEM((1,), jnp.int32),
             pltpu.VMEM((q_heads, rows, HEAD), jnp.bfloat16),
             pltpu.VMEM((kv_heads, rows, HEAD), jnp.bfloat16),
             pltpu.VMEM((kv_heads, window * rows, HEAD), jnp.bfloat16),
@@ -324,15 +335,13 @@
             pltpu.VMEM((rows, 2 * rows), jnp.float32),
             pltpu.VMEM((q_heads, rows, LANES), jnp.float32),
             pltpu.VMEM((q_heads, rows, 2 * HEAD), jnp.float32),
-            pltpu.VMEM(queries.shape, jnp.bfloat16),
             pltpu.VMEM((rows, HEAD), jnp.float32),
             pltpu.VMEM((1, wide), jnp.float32),
             pltpu.VMEM((1, wide), jnp.float32),
             pltpu.SemaphoreType.DMA((3, window, chunks)),
             pltpu.SemaphoreType.DMA((window, chunks)),
-            pltpu.SemaphoreType.DMA((1 + kv_heads,)),
             pltpu.SemaphoreType.DMA((2,)),
-            pltpu.SemaphoreType.DMA((5,)),
+            pltpu.SemaphoreType.DMA((6,)),
         ],
         compiler_params=pltpu.CompilerParams(
             collective_id=0, has_side_effects=True, vmem_limit_bytes=60 * 1024 * 1024

time: 29 us -> 23.7 us (0.82)
  Pallas kernels: 24.9 us -> 19.6 us
    pallas_call x1, Pallas kernels: 24.9 us -> 19.6 us  [per_device(): pl.pallas_call(functools.partial(kernel, n, window, ways), out_shape=(jax...]
where the time goes in v3:
time: 23.7 us; the launch traced here: 23.6 us
  Pallas kernels  19.6 us (83%)
  local copies, waits for them, and re-layouts  2.66 us (11%)
  between operations  1.29 us (5%)
    pallas_call x1, Pallas kernels, per_device(): pl.pallas_call(functools.partial(kernel, n, window, ways), out_shape=(jax...  19.6 us
    unnamed x4, local copies, waits for them, and re-layouts  2.66 us

profile of v3, /device:TPU:17, one launch (start us, length us, event | category | flops | bytes accessed | tf_op | source)
XLA Modules:
  0.0 23.6 jit_solution(11817609558259427522)
XLA Ops:
  1.3 19.6 %shard_map.77 = (bf16[192,2048]{1,0:T(8,128)(2,1)}, f32[1,192]{1,0:T(1,128)}) custom-call(bf16[192,2048]{1,0:T(8,128)(2,1)} %q_hbm.1, bf16[192,256]{1,0:T(8,128)(2,1)} %k_hbm.1, bf16[192,256]{1,0:T(8,128)(2,1)} %v_hbm.1, s32[1,192]{1,0:T(1,128)} %bitcast.5, s32[1]{0:T(128)S(6)} %copy.10.valid_hbm, f32[16,128]{1,0:T(8,128)} %bitcast.3), custom_call_target="tpu_custom_call" | custom-call | tf_op jit(solution)/shard_map/pallas_call | solution.py:307
  20.9 0.0 copy-start
  20.9 2.1 %copy.11 = bf16[192,2048]{1,0:T(8,128)(2,1)} copy(bf16[192,2048]{1,0:T(8,128)(2,1)} %get-tuple-element.8) | data formatting | bytes 1572864
  23.0 0.0 copy-done
  23.0 0.6 %copy.12 = f32[192]{0:T(256)} copy(f32[192]{0:T(256)S(1)} %bitcast.4) | data formatting | bytes 1536
Async XLA Ops:
  20.9 2.1 %copy-start = (f32[1,192]{1,0:T(1,128)S(1)}, f32[1,192]{1,0:T(1,128)}, u32[]{:S(2)}) copy-start(f32[1,192]{1,0:T(1,128)} %get-tuple-element.5) | copy-start | bytes 2308

commit v4 on v3

--- a/solution.py
+++ b/solution.py
@@ -15,6 +15,8 @@
 BLOCKED = -1e30
 BATCH = 4
 PART = 96
+PIECES = 1
+COPIES = 4
 
 
 def kernel(
@@ -27,7 +29,7 @@
     seg_hbm,
     valid_hbm,
     weight_hbm,
-    out_buf,
+    out_hbm,
     reward_ref,
     q_in,
     k_ref,
@@ -44,6 +46,7 @@
     bias_ref,
     max_ref,
     acc_ref,
+    out_buf,
     rew_acc,
     rew_own,
     rew_far,
@@ -51,12 +54,13 @@
     recv_sem,
     rew_sem,
     load_sem,
+    store_sem,
 ):
     rows = k_ref.shape[0]
     kv_heads = k_ref.shape[1] // HEAD
     q_heads = q_in.shape[1] // HEAD
     group = q_heads // kv_heads
-    chunks = 1 + 2 * kv_heads
+    chunks = 1 + 2 * kv_heads * PIECES
     me = lax.axis_index("ctx")
     other = 1 - lax.axis_index("tp")
     odd = lax.rem(me, 2)
@@ -80,27 +84,33 @@
         loads.append(pltpu.make_async_copy(source, target, load_sem.at[at]))
         loads[-1].start()
 
-    def outgoing(slot):
+    def outgoing(slot, chunk):
         held = me - 1 - slot >= 0
         if ways == 1:
             return [(0, slot + 1, me + 1, held & (me + 1 < n))] if slot + 1 < window else []
         sends = []
+        late = chunk == chunks - 1
         if slot == -1 or slot % 2 == 1:
             if slot + 2 < window:
                 sends.append((0, slot + 2, me + 2, held & (me + 2 < n)))
             if slot + 1 < window:
                 sends.append((1, slot + 1, me + 1, held & (odd == 0)))
-            if slot >= 1:
+            if slot == 1 or (slot > 1 and not late):
                 sends.append((2, slot - 1, me - 1, held & (odd == 1)))
+        elif late and slot + 2 < window:
+            sends.append((2, slot + 2, me + 2, held & (odd == 0) & (me + 2 < n)))
         return sends
 
     def piece(slot, chunk):
         if chunk == 0:
             return seg_own if slot < 0 else seg_buf.at[slot]
-        head, is_key = (chunk - 1) // 2, (chunk - 1) % 2 == 1
+        which, part = (chunk - 1) // PIECES, (chunk - 1) % PIECES
+        head, is_key = which // 2, which % 2 == 1
+        size = rows // PIECES
         if slot < 0:
-            return k_own.at[head] if is_key else v_ref.at[:, pl.ds(head * HEAD, HEAD)]
-        return (k_buf if is_key else v_buf).at[head, pl.ds(slot * rows, rows)]
+            own = pl.ds(part * size, size)
+            return k_own.at[head, own] if is_key else v_ref.at[own, pl.ds(head * HEAD, HEAD)]
+        return (k_buf if is_key else v_buf).at[head, pl.ds(slot * rows + part * size, size)]
 
     def copy_of(slot, chunk, path, there, device):
         return pltpu.make_async_remote_copy(
@@ -113,29 +123,29 @@
         )
 
     def send(slot, chunk):
-        for path, there, device, condition in outgoing(slot):
+        for path, there, device, condition in outgoing(slot, chunk):
             @pl.when(condition)
             def _(path=path, there=there, device=device):
                 copy_of(slot, chunk, path, there, device).start()
 
     def finish_send(slot, chunk):
-        for path, there, device, condition in outgoing(slot):
+        for path, there, device, condition in outgoing(slot, chunk):
             @pl.when(condition)
             def _(path=path, there=there, device=device):
                 copy_of(slot, chunk, path, there, device).wait_send()
 
     arrived = set()
 
-    def arrive(slot, chunk):
-        if slot >= window or chunk >= chunks or (slot, chunk) in arrived:
+    def arrive(slot, which):
+        if slot >= window or which > 2 * kv_heads or (slot, which) in arrived:
             return
-        arrived.add((slot, chunk))
-
-        @pl.when(me - 1 - slot >= 0)
-        def _():
-            copy_of(slot, chunk, 0, slot, me).wait_recv()
-
-        send(slot, chunk)
+        arrived.add((slot, which))
+        for chunk in (0,) if which == 0 else range(1 + (which - 1) * PIECES, 1 + which * PIECES):
+            @pl.when(me - 1 - slot >= 0)
+            def _(chunk=chunk):
+                copy_of(slot, chunk, 0, slot, me).wait_recv()
+
+            send(slot, chunk)
 
     for slot in range(window):
         @pl.when(me - 1 - slot < 0)
@@ -247,6 +257,7 @@
     rew_acc[...] = jnp.zeros_like(rew_acc)
     stages = window // 2
     lane_at = lax.broadcasted_iota(jnp.int32, (1, 2 * rows), 1)
+    stores = []
     second = (lane_at >= rows).astype(jnp.int32)
     for stage in range(stages):
         near, far = 2 * stage, 2 * stage + 1
@@ -265,6 +276,15 @@
             steps = group // per_step
             for step in range(steps):
                 later(stage, kv, step, last)
+                if last:
+                    head0 = kv * group + step * per_step
+                    columns = pl.ds(head0 * HEAD, per_step * HEAD)
+                    stores.append(
+                        pltpu.make_async_copy(
+                            out_buf.at[:, columns], out_hbm.at[:, columns], store_sem.at[head0 // per_step]
+                        )
+                    )
+                    stores[-1].start()
                 ahead = 2 * stage + lead + (0 if kv + 1 < kv_heads else 2)
                 after = 1 + 2 * (kv + 1) if kv + 1 < kv_heads else 1
                 if ahead > 2 * stage + 1:
@@ -290,6 +310,29 @@
             finish_send(slot, chunk)
     swap.wait()
     reward_ref[...] = mine_row + rew_far[:, :rows]
+    for store in stores:
+        store.wait()
+
+
+def hand_over(out_near, rew_near, out_far, rew_far, out_stage, rew_stage, load_sem, store_sem):
+    size = out_near.shape[0] // COPIES
+    moves = [(rew_near, rew_stage, rew_far)]
+    for at in range(COPIES):
+        span = pl.ds(at * size, size)
+        moves.append((out_near.at[span], out_stage.at[span], out_far.at[span]))
+    loads = [
+        pltpu.make_async_copy(near, stage, load_sem.at[at]) for at, (near, stage, far) in enumerate(moves)
+    ]
+    stores = [
+        pltpu.make_async_copy(stage, far, store_sem.at[at]) for at, (near, stage, far) in enumerate(moves)
+    ]
+    for load in loads:
+        load.start()
+    for load, store in zip(loads, stores):
+        load.wait()
+        store.start()
+    for store in stores:
+        store.wait()
 
 
 def per_device(n, queries, keys, values, segments, valid_length, reward_weight):
@@ -300,7 +343,7 @@
     window = -(-(span - 1) // rows)
     window += window % 2
     ways = 2 if n <= 8 else 1
-    chunks = 1 + 2 * kv_heads
+    chunks = 1 + 2 * kv_heads * PIECES
     wide = -(-rows // LANES) * LANES
     vmem = pl.BlockSpec(memory_space=pltpu.VMEM)
     hbm = pl.BlockSpec(memory_space=pltpu.HBM)
@@ -318,7 +361,7 @@
             hbm,
             hbm,
         ],
-        out_specs=(vmem, vmem),
+        out_specs=(hbm, vmem),
         scratch_shapes=[
             pltpu.VMEM(queries.shape, jnp.bfloat16),
             pltpu.VMEM(keys.shape, jnp.bfloat16),
@@ -335,6 +378,7 @@
             pltpu.VMEM((rows, 2 * rows), jnp.float32),
             pltpu.VMEM((q_heads, rows, LANES), jnp.float32),
             pltpu.VMEM((q_heads, rows, 2 * HEAD), jnp.float32),
+            pltpu.VMEM(queries.shape, jnp.bfloat16),
             pltpu.VMEM((rows, HEAD), jnp.float32),
             pltpu.VMEM((1, wide), jnp.float32),
             pltpu.VMEM((1, wide), jnp.float32),
@@ -342,6 +386,7 @@
             pltpu.SemaphoreType.DMA((window, chunks)),
             pltpu.SemaphoreType.DMA((2,)),
             pltpu.SemaphoreType.DMA((6,)),
+            pltpu.SemaphoreType.DMA((q_heads // 4,)),
         ],
         compiler_params=pltpu.CompilerParams(
             collective_id=0, has_side_effects=True, vmem_limit_bytes=60 * 1024 * 1024
@@ -354,6 +399,22 @@
         valid_length,
         reward_weight.reshape(q_heads, HEAD),
     )
+    attention, reward = pl.pallas_call(
+        hand_over,
+        out_shape=(
+            jax.ShapeDtypeStruct(queries.shape, jnp.bfloat16),
+            jax.ShapeDtypeStruct((1, rows), jnp.float32),
+        ),
+        in_specs=[hbm, hbm],
+        out_specs=(hbm, hbm),
+        scratch_shapes=[
+            pltpu.VMEM(queries.shape, jnp.bfloat16),
+            pltpu.VMEM((1, rows), jnp.float32),
+            pltpu.SemaphoreType.DMA((COPIES + 1,)),
+            pltpu.SemaphoreType.DMA((COPIES + 1,)),
+        ],
+        compiler_params=pltpu.CompilerParams(vmem_limit_bytes=60 * 1024 * 1024),
+    )(attention, reward)
     return attention, reward.reshape(rows)
 
 

time: 23.7 us -> 22.7 us (0.958)
  local copies, waits for them, and re-layouts: 2.66 us -> 0 us
  Pallas kernels: 19.6 us -> 21.3 us
    unnamed x4 -> x0, local copies, waits for them, and re-layouts: 2.66 us -> none
    pallas_call x0 -> x1, Pallas kernels: none -> 1.99 us  [per_device(): pl.pallas_call(hand_over, out_shape=(jax.ShapeDtypeStruct(queries.shape,...]
    pallas_call x1, Pallas kernels: 19.6 us -> 19.3 us  [per_device(): pl.pallas_call(functools.partial(kernel, n, window, ways), out_shape=(jax...]
where the time goes in v4:
time: 22.7 us; the launch traced here: 22.6 us
  Pallas kernels  21.3 us (94%)
  between operations  1.29 us (6%)
    pallas_call x1, Pallas kernels, per_device(): pl.pallas_call(functools.partial(kernel, n, window, ways), out_shape=(jax...  19.3 us
    pallas_call x1, Pallas kernels, per_device(): pl.pallas_call(hand_over, out_shape=(jax.ShapeDtypeStruct(queries.shape,...  1.99 us

profile of v4, /device:TPU:17, one launch (start us, length us, event | category | flops | bytes accessed | tf_op | source)
XLA Modules:
  0.0 22.6 jit_solution(13227692170131882215)
XLA Ops:
  1.3 19.3 %shard_map.77 = (bf16[192,2048]{1,0:T(8,128)(2,1)}, f32[1,192]{1,0:T(1,128)}) custom-call(bf16[192,2048]{1,0:T(8,128)(2,1)} %q_hbm.1, bf16[192,256]{1,0:T(8,128)(2,1)} %k_hbm.1, bf16[192,256]{1,0:T(8,128)(2,1)} %v_hbm.1, s32[1,192]{1,0:T(1,128)} %bitcast.4, s32[1]{0:T(128)S(6)} %copy.8.valid_hbm, f32[16,128]{1,0:T(8,128)} %bitcast.3), custom_call_target="tpu_custom_call" | custom-call | tf_op jit(solution)/shard_map/pallas_call | solution.py:350
  20.6 2.0 %shard_map.78 = (bf16[192,2048]{1,0:T(8,128)(2,1)}, f32[1,192]{1,0:T(1,128)}) custom-call(bf16[192,2048]{1,0:T(8,128)(2,1)} %get-tuple-element.6.out_near, f32[1,192]{1,0:T(1,128)} %get-tuple-element.7.rew_near), custom_call_target="tpu_custom_call" | custom-call | tf_op jit(solution)/shard_map/pallas_call | solution.py:402

commit v5 on v4

--- a/solution.py
+++ b/solution.py
@@ -13,7 +13,7 @@
 MESH = pl.DeviceIdType.MESH
 SCALE = HEAD**-0.5 * math.log2(math.e)
 BLOCKED = -1e30
-BATCH = 4
+BATCH = 8
 PART = 96
 PIECES = 1
 COPIES = 4
@@ -122,8 +122,11 @@
             device_id_type=MESH,
         )
 
-    def send(slot, chunk):
+    def send(slot, chunk, paths=(0, 1, 2)):
         for path, there, device, condition in outgoing(slot, chunk):
+            if path not in paths:
+                continue
+
             @pl.when(condition)
             def _(path=path, there=there, device=device):
                 copy_of(slot, chunk, path, there, device).start()
@@ -179,8 +182,9 @@
         barrier, ways + (me + ways < n).astype(jnp.int32) + (me >= ways).astype(jnp.int32)
     )
 
-    for chunk in range(chunks):
-        send(-1, chunk)
+    for path in range(2):
+        for chunk in range(chunks):
+            send(-1, chunk, (path,))
 
     loads[3].wait()
     for head in range(q_heads):
@@ -223,7 +227,7 @@
     causal = (seg_row == seg_col) & (col_at <= row_at)
     causal = causal & ((me * rows + col_at < valid) | (col_at == row_at))
     bias_ref[:, :rows] = jnp.where(causal, 0.0, BLOCKED)
-    per_step = min(4, group)
+    per_step = min(8, group)
 
     def keep(head0, results):
         for i, r, top, mixed in results:
@@ -231,7 +235,7 @@
             max_ref[head0 + i, r : r + PART] = top
 
     lead = ways - 1
-    polls = [(0,), (1,), (2,), ()]
+    polls = [(), (0, 1)]
     for kv in range(kv_heads):
         for step in range(group // per_step):
             here = kv * group + step * per_step
@@ -386,7 +390,7 @@
             pltpu.SemaphoreType.DMA((window, chunks)),
             pltpu.SemaphoreType.DMA((2,)),
             pltpu.SemaphoreType.DMA((6,)),
-            pltpu.SemaphoreType.DMA((q_heads // 4,)),
+            pltpu.SemaphoreType.DMA((q_heads // 8,)),
         ],
         compiler_params=pltpu.CompilerParams(
             collective_id=0, has_side_effects=True, vmem_limit_bytes=60 * 1024 * 1024

time: 22.7 us -> 22.2 us (0.978)
  Pallas kernels: 21.3 us -> 20.8 us
    pallas_call x1, Pallas kernels: 19.3 us -> 18.8 us  [per_device(): pl.pallas_call(functools.partial(kernel, n, window, ways), out_shape=(jax...]
where the time goes in v5:
time: 22.2 us; the launch traced here: 22.1 us
  Pallas kernels  20.8 us (94%)
  between operations  1.29 us (6%)
    pallas_call x1, Pallas kernels, per_device(): pl.pallas_call(functools.partial(kernel, n, window, ways), out_shape=(jax...  18.8 us
    pallas_call x1, Pallas kernels, per_device(): pl.pallas_call(hand_over, out_shape=(jax.ShapeDtypeStruct(queries.shape,...  1.99 us

profile of v5, /device:TPU:17, one launch (start us, length us, event | category | flops | bytes accessed | tf_op | source)
XLA Modules:
  0.0 22.1 jit_solution(715973889811085678)
XLA Ops:
  1.3 18.8 %shard_map.77 = (bf16[192,2048]{1,0:T(8,128)(2,1)}, f32[1,192]{1,0:T(1,128)}) custom-call(bf16[192,2048]{1,0:T(8,128)(2,1)} %q_hbm.1, bf16[192,256]{1,0:T(8,128)(2,1)} %k_hbm.1, bf16[192,256]{1,0:T(8,128)(2,1)} %v_hbm.1, s32[1,192]{1,0:T(1,128)} %bitcast.4, s32[1]{0:T(128)S(6)} %copy.8.valid_hbm, f32[16,128]{1,0:T(8,128)} %bitcast.3), custom_call_target="tpu_custom_call" | custom-call | tf_op jit(solution)/shard_map/pallas_call | solution.py:354
  20.1 2.0 %shard_map.78 = (bf16[192,2048]{1,0:T(8,128)(2,1)}, f32[1,192]{1,0:T(1,128)}) custom-call(bf16[192,2048]{1,0:T(8,128)(2,1)} %get-tuple-element.6.out_near, f32[1,192]{1,0:T(1,128)} %get-tuple-element.7.rew_near), custom_call_target="tpu_custom_call" | custom-call | tf_op jit(solution)/shard_map/pallas_call | solution.py:406
